TPU v7x, 128 devices: a whole 4x4x4 slice. The times are simulated.
128 devices in a mesh: seq: 16 (over y, x_lo, core), tp: 8 (over z, x_hi).
Axes of the slice: x: 4 (x_hi: 2, x_lo: 2; x = x_hi * 2 + x_lo), y: 4, z: 4, core: 2. Of those that a mesh axis runs over, the one named last changes fastest.
Arguments:
- grad_out: bfloat16 [32768, 8192], P('seq', 'tp'), may hold values from -6 to 6
- select: int32 [4096], P('seq'), may hold values from 0 to 2047, as said below
- router: float32 [4096], P('seq'), may hold values from 0.1 to 1
- query: bfloat16 [4096, 8192], P('seq', 'tp'), may hold values from -7 to 7
- key_rows: bfloat16 [4096, 1024], P('seq', 'tp'), may hold values from -6 to 6
- value_rows: bfloat16 [4096, 1024], P('seq', 'tp'), may hold values from -6 to 6
- out_weight: bfloat16 [8192, 8192], P('tp'), may hold values from -0.0625 to 0.0625
Outputs:
- grad_query: bfloat16 [4096, 8192], P('seq', 'tp')
- grad_key: bfloat16 [4096, 1024], P('seq', 'tp')
- grad_value: bfloat16 [4096, 1024], P('seq', 'tp')
- grad_router: float32 [4096], P('seq')
Inputs may be any that keep to these rules, and one draw needn't show every extreme that they name: `select`: within each aligned block of 256 rows (one sequence shard) the positions are distinct and increasing, and every block holds its shard's first and last token.
All inputs are finite; a program needn't handle non-finite values.
Results may differ from a plain program's by a relative error of at most 0.008.
Values may be sent and summed in bfloat16 or wider, within the bound.
A program may use at most 192 MiB of HBM per device.

v0:
```python
import math

import jax
import jax.numpy as jnp
from jax import lax
from jax.sharding import PartitionSpec as P

HEADS = 64
KV_HEADS = 8
HD = 128


FLOOR_START = -1e30


def split_query(flat):
    group = HEADS // KV_HEADS
    return flat.reshape(flat.shape[0], flat.shape[1] // (group * HD), group, HD)


def split_pairs(flat):
    return flat.reshape(flat.shape[0], flat.shape[1] // HD, HD)


def keep_state(state_now):
    return state_now


def masked_scores(queries, key_block, query_places, key_places, factor):
    scores = (
        jnp.einsum("qagd,kad->agqk", queries, key_block, preferred_element_type=jnp.float32)
        * factor
    )
    allowed = key_places[None, None, None, :] <= query_places[None, None, :, None]
    return (scores, allowed)


def stats_update(state_now, queries, query_places, key_block, key_places, factor):
    running_top, running_total = state_now
    scores, allowed = masked_scores(queries, key_block, query_places, key_places, factor)
    new_top = jnp.maximum(running_top, jnp.max(jnp.where(allowed, scores, FLOOR_START), axis=3))
    weights = jnp.where(allowed, jnp.exp(scores - new_top[:, :, :, None]), 0.0)
    return (new_top, jnp.sum(weights, axis=3))


def values_update(queries, query_places, logs, key_block, values, key_places, factor):
    scores, allowed = masked_scores(queries, key_block, query_places, key_places, factor)
    weights = jnp.where(allowed, jnp.exp(scores - logs[:, :, :, None]), 0.0).astype(jnp.bfloat16)
    return jnp.einsum("agqk,kad->agqd", weights, values, preferred_element_type=jnp.float32)


def backward_terms(
    queries,
    gradients,
    query_places,
    log_totals,
    deltas,
    key_block,
    values,
    key_places,
    factor,
    wanted,
):
    scores, allowed = masked_scores(queries, key_block, query_places, key_places, factor)
    probabilities = jnp.where(allowed, jnp.exp(scores - log_totals[:, :, :, None]), 0.0)
    grad_probs = jnp.einsum("qagd,kad->agqk", gradients, values, preferred_element_type=jnp.float32)
    grad_scores = (probabilities * (grad_probs - deltas[:, :, :, None])).astype(jnp.bfloat16)
    if wanted == "queries":
        return (
            jnp.einsum("agqk,kad->qagd", grad_scores, key_block, preferred_element_type=jnp.float32)
            * factor
        )
    grad_keys = (
        jnp.einsum("agqk,qagd->kad", grad_scores, queries, preferred_element_type=jnp.float32)
        * factor
    )
    grad_values = jnp.einsum(
        "agqk,qagd->kad",
        probabilities.astype(jnp.bfloat16),
        gradients,
        preferred_element_type=jnp.float32,
    )
    return (grad_keys, grad_values)


def body(grad_out, select, router, query, key_rows, value_rows, out_weight):
    rows_here = select.shape[0]
    half_rows = rows_here // 2
    feature_width = query.shape[1]
    pair_width = key_rows.shape[1]
    pair_count = pair_width // HD
    group = HEADS // KV_HEADS
    factor = 1.0 / math.sqrt(HD)
    places = lax.axis_index("seq") * grad_out.shape[0] + select
    picked = jnp.take(grad_out, select, axis=0)
    picked_full = lax.all_gather(picked, "tp", axis=1, tiled=True)
    grad_block = (router[:, None] * picked_full.astype(jnp.float32)).astype(jnp.bfloat16)
    grad_attended = lax.dot_general(
        grad_block, out_weight, (((1,), (1,)), ((), ())), preferred_element_type=jnp.float32
    ).astype(jnp.bfloat16)
    query_heads = split_query(query)
    grad_heads = split_query(grad_attended)
    section_list = []
    for section in range(2):
        lower_row = section * half_rows
        section_list.append(
            (
                query_heads[lower_row : lower_row + half_rows],
                grad_heads[lower_row : lower_row + half_rows],
                places[lower_row : lower_row + half_rows],
            )
        )
    start_state = (
        jnp.full((pair_count, group, half_rows), FLOOR_START, jnp.float32),
        jnp.zeros((pair_count, group, half_rows), jnp.float32),
    )
    carried = (start_state, start_state)
    arrived = (
        lax.all_gather(key_rows, "seq", axis=0, tiled=True),
        lax.all_gather(places, "seq", axis=0, tiled=True),
    )
    key_block = split_pairs(arrived[0])
    key_places = arrived[1]
    updated = []
    for section in range(2):
        section_queries, section_grads, section_places = section_list[section]

        def stats_advance(
            state_now, section_queries=section_queries, section_places=section_places
        ):
            return stats_update(
                state_now, section_queries, section_places, key_block, key_places, factor
            )

        updated.append(
            lax.cond(
                jnp.min(key_places) > jnp.max(section_places),
                keep_state,
                stats_advance,
                carried[section],
            )
        )
    stats = tuple(updated)
    section_logs_list = [stats[0][0] + jnp.log(stats[0][1]), stats[1][0] + jnp.log(stats[1][1])]
    log_totals = jnp.concatenate(section_logs_list, axis=2)
    sum_zero = jnp.zeros((pair_count, group, half_rows, HD), jnp.float32)
    carried = (sum_zero, sum_zero)
    arrived = (
        lax.all_gather(key_rows, "seq", axis=0, tiled=True),
        lax.all_gather(value_rows, "seq", axis=0, tiled=True),
        lax.all_gather(places, "seq", axis=0, tiled=True),
    )
    values_key_block = split_pairs(arrived[0])
    values = split_pairs(arrived[1])
    values_key_places = arrived[2]
    updated = []
    for section in range(2):
        section_queries, section_grads, section_places = section_list[section]
        section_logs = section_logs_list[section]

        def values_advance(
            state_now,
            section_queries=section_queries,
            section_places=section_places,
            section_logs=section_logs,
        ):
            return values_update(
                section_queries,
                section_places,
                section_logs,
                values_key_block,
                values,
                values_key_places,
                factor,
            )

        updated.append(
            lax.cond(
                jnp.min(values_key_places) > jnp.max(section_places),
                keep_state,
                values_advance,
                carried[section],
            )
        )
    summed = tuple(updated)
    attended_heads = jnp.concatenate([summed[0], summed[1]], axis=2).astype(jnp.bfloat16)
    attended_set = attended_heads.transpose(2, 0, 1, 3).reshape(rows_here, feature_width)
    deltas = jnp.sum(
        split_query(attended_set).astype(jnp.float32) * grad_heads.astype(jnp.float32), axis=3
    ).transpose(1, 2, 0)
    arrived = (
        lax.all_gather(key_rows, "seq", axis=0, tiled=True),
        lax.all_gather(value_rows, "seq", axis=0, tiled=True),
        lax.all_gather(places, "seq", axis=0, tiled=True),
    )
    query_key_block = split_pairs(arrived[0])
    query_values = split_pairs(arrived[1])
    query_key_places = arrived[2]
    query_parts = []
    for section in range(2):
        section_queries, section_grads, section_places = section_list[section]
        section_logs = log_totals[:, :, section * half_rows : (section + 1) * half_rows]
        section_deltas = deltas[:, :, section * half_rows : (section + 1) * half_rows]

        def query_contribute(
            section_queries=section_queries,
            section_grads=section_grads,
            section_places=section_places,
            section_logs=section_logs,
            section_deltas=section_deltas,
        ):
            return backward_terms(
                section_queries,
                section_grads,
                section_places,
                section_logs,
                section_deltas,
                query_key_block,
                query_values,
                query_key_places,
                factor,
                "queries",
            )

        def query_nothing():
            return jnp.zeros((half_rows, pair_count, group, HD), jnp.float32)

        query_parts.append(
            lax.cond(
                jnp.min(query_key_places) > jnp.max(section_places), query_nothing, query_contribute
            )
        )
    query_grads = tuple(query_parts)
    logs_flat = log_totals.transpose(2, 0, 1).reshape(rows_here, pair_count * group)
    deltas_flat = deltas.transpose(2, 0, 1).reshape(rows_here, pair_count * group)
    all_logs, all_deltas = (
        lax.all_gather(logs_flat, "seq", axis=0, tiled=True),
        lax.all_gather(deltas_flat, "seq", axis=0, tiled=True),
    )
    own_keys = split_pairs(key_rows)
    own_values = split_pairs(value_rows)
    own_zero = jnp.zeros((rows_here, pair_count, HD), jnp.float32)
    carried = (own_zero, own_zero)
    arrived = (
        lax.all_gather(query, "seq", axis=0, tiled=True),
        lax.all_gather(grad_attended, "seq", axis=0, tiled=True),
        lax.all_gather(places, "seq", axis=0, tiled=True),
    )
    row_count = arrived[0].shape[0]
    piece_logs = all_logs.reshape(row_count, pair_count, group).transpose(1, 2, 0)
    piece_deltas = all_deltas.reshape(row_count, pair_count, group).transpose(1, 2, 0)

    def key_contribute():
        return backward_terms(
            split_query(arrived[0]),
            split_query(arrived[1]),
            arrived[2],
            piece_logs,
            piece_deltas,
            own_keys,
            own_values,
            places,
            factor,
            "keys",
        )

    def key_nothing():
        return (jnp.zeros_like(carried[0]), jnp.zeros_like(carried[1]))

    grad_k_part, grad_v_part = lax.cond(
        jnp.max(arrived[2]) < jnp.min(places), key_nothing, key_contribute
    )
    grad_key = grad_k_part.reshape(rows_here, pair_width).astype(jnp.bfloat16)
    grad_value = grad_v_part.reshape(rows_here, pair_width).astype(jnp.bfloat16)
    grad_query_set = (
        jnp.concatenate([query_grads[0], query_grads[1]], axis=0)
        .reshape(rows_here, feature_width)
        .astype(jnp.bfloat16)
    )
    block_part = jnp.dot(attended_set, out_weight, preferred_element_type=jnp.float32)
    router_term = jnp.sum(picked_full.astype(jnp.float32) * block_part, axis=1)
    grad_router = lax.psum(router_term, "tp")
    return (grad_query_set, grad_key, grad_value, grad_router)


def solution(mesh):
    return jax.shard_map(
        body,
        mesh=mesh,
        in_specs=(
            P("seq", "tp"),
            P("seq"),
            P("seq"),
            P("seq", "tp"),
            P("seq", "tp"),
            P("seq", "tp"),
            P("tp", None),
        ),
        out_specs=(P("seq", "tp"), P("seq", "tp"), P("seq", "tp"), P("seq")),
        check_vma=False,
    )
```

profile of v0, /device:TPU:1, one launch (start us, length us, event | category | flops | bytes accessed | tf_op | source)
XLA Modules:
  0.0 398.4 jit_solution(12879807301170258821)
XLA Ops:
  9.2 4.3 %gather_fusion = bf16[256,1024]{1,0:T(8,128)(2,1)S(1)} fusion(bf16[2048,1024]{1,0:T(8,128)(2,1)} %param.21, s32[1024]{0:T(1024)S(1)} %pad_clamp_fusion), kind=kCustom, calls=%fused_computation | custom fusion | bytes 1049600 | tf_op jit(solution)/shard_map/jit(_take)/gather | solution.py:95
  16.6 72.4 %all-gather.12.cloned.1.call-done = bf16[256,8192]{1,0:T(8,128)(2,1)} async-done(((bf16[256,1024]{1,0:T(8,128)(2,1)}), bf16[256,8192]{1,0:T(8,128)(2,1)}) %all-gather.12.cloned.1.call-update) | async-done | bytes 4194320 | tf_op jit(solution)/shard_map/all_gather | solution.py:96
  89.0 12.4 %fusion.171 = bf16[256,1024]{1,0:T(8,128)(2,1)} fusion(bf16[1024,8192]{1,0:T(8,128)(2,1)} %param.27, bf16[256,8192]{1,0:T(8,128)(2,1)} %all-gather.12.cloned.1.call-done, f32[256]{0:T(256)} %param.23), kind=kOutput, calls=%fused_computation.144 | convolution fusion | flops 4301520896 | bytes 21496832 | tf_op jit(solution)/shard_map/dot_general | solution.py:98
  101.4 19.6 %all-gather.1 = s32[16,1,256]{2,1,0:T(1,128)S(1)} all-gather(s32[1,1,256]{2,1,0:T(1,128)S(1)} %bitcast.456), channel_id=1, replica_groups=mesh['seq'=16,'tp'=8] {'seq'}, dimensions={0}, use_global_device_ids=true | all-gather | bytes 17408 | tf_op jit(solution)/shard_map/all_gather | solution.py:194
  126.7 19.9 %conditional.7 = (f32[1,8,128]{2,1,0:T(8,128)S(1)}, f32[1,8,128]{2,1,0:T(8,128)S(1)}) conditional(s32[]{:T(128)} %convert_element_type.86, (s32[4096]{0:T(1024)S(1)}, s32[128]{0:T(128)S(1)}, bf16[4096,1,128]{2,0,1:T(8,128)(2,1)}, bf16[128,1,8,128]{0,3,2,1:T(8,128)(2,1)S(1)}) %tuple.145, () %tuple.65), branch_computations={%region_2.0_spmd, %region_5.6_spmd} | conditional | flops 1103625216 | bytes 36487696 | solution.py:136
  127.1 1.9 broadcast_compare_fusion
  129.0 8.2 %fusion = (f32[8,128]{1,0:T(8,128)S(1)}, f32[4096,128,8]{1,0,2:T(8,128)}) fusion(pred[128,4096]{0,1:T(8,128)(4,1)S(1)} %broadcast_compare_fusion, bf16[128,1,8,128]{0,3,2,1:T(8,128)(2,1)S(1)} %get-tuple-element.211, bf16[4096,1,128]{2,0,1:T(8,128)(2,1)} %get-tuple-element.114), kind=kOutput, calls=%fused_computation.3 | convolution fusion | flops 1086323712 | bytes 18616320 | tf_op jit(solution)/shard_map/cond/branch_0_fun/qagd,kad->agqk/dot_general | solution.py:31
  137.3 9.3 %fusion.3 = f32[8,128]{1,0:T(8,128)S(1)} fusion(f32[4096,128,8]{1,0,2:T(8,128)} %get-tuple-element.253, f32[8,128]{1,0:T(8,128)S(1)} %get-tuple-element.250, pred[128,4096]{0,1:T(8,128)(4,1)S(1)} %broadcast_compare_fusion), kind=kLoop, calls=%fused_computation.6 | loop fusion | flops 16776192 | bytes 17309696 | tf_op jit(solution)/shard_map/cond/branch_0_fun/reduce_sum | solution.py:43
  146.6 9.4 %all-gather.10.cloned.1.call-done = bf16[4096,128]{1,0:T(8,128)(2,1)} async-done(((bf16[256,128]{1,0:T(8,128)(2,1)}), bf16[4096,128]{1,0:T(8,128)(2,1)}) %all-gather.10.cloned.1.call-update) | async-done | bytes 1048592 | tf_op jit(solution)/shard_map/all_gather | solution.py:193
  156.0 11.3 %conditional.8 = (bf16[1,8,128,128]{3,2,1,0:T(8,128)(2,1)S(1)}) conditional(s32[]{:T(128)} %convert_element_type.86, (s32[4096]{0:T(1024)S(1)}, s32[128]{0:T(128)S(1)}, bf16[4096,1,128]{2,0,1:T(8,128)(2,1)}, bf16[128,1,8,128]{0,3,2,1:T(8,128)(2,1)S(1)}, f32[1,8,128]{2,1,0:T(8,128)S(1)}, /*index=5*/bf16[4096,1,128]{2,0,1:T(8,128)(2,1)}) %tuple.146, () %tuple.67), branch_computations={%region_6.7_spmd, %region_7.8_spmd} | conditional | flops 2164785152 | bytes 3691016 | solution.py:178
  158.0 9.3 %fusion.17 = bf16[1,8,128,128]{3,2,1,0:T(8,128)(2,1)S(1)} fusion(f32[8,128]{1,0:T(8,128)S(1)} %bitcast.457, pred[128,4096]{0,1:T(8,128)(4,1)S(1)} %broadcast_compare_fusion.1, bf16[4096,1,128]{2,0,1:T(8,128)(2,1)} %get-tuple-element.121, bf16[4096,1,128]{2,0,1:T(8,128)(2,1)} %get-tuple-element.118, bf16[128,1,8,128]{0,3,2,1:T(8,128)(2,1)S(1)} %get-tuple-element.215), kind=kOutput, calls=%fused_computation.24 | convolution fusion | flops 2164260864 | bytes 3149824 | tf_op jit(solution)/shard_map/cond/branch_0_fun/agqk,kad->agqd/dot_general | solution.py:49
  167.5 20.1 %conditional.9 = (f32[1,8,128]{2,1,0:T(8,128)S(1)}, f32[1,8,128]{2,1,0:T(8,128)S(1)}) conditional(s32[]{:T(128)} %convert_element_type.90, (s32[4096]{0:T(1024)S(1)}, s32[128]{0:T(128)S(1)}, bf16[4096,1,128]{2,0,1:T(8,128)(2,1)}, bf16[128,1,8,128]{0,3,2,1:T(8,128)(2,1)S(1)}) %tuple.148, () %tuple.69), branch_computations={%region_9.12_spmd, %region_12.13_spmd} | conditional | flops 1103625216 | bytes 36487696 | solution.py:136
  169.7 8.5 %fusion.27 = (f32[8,128]{1,0:T(8,128)S(1)}, f32[4096,128,8]{1,0,2:T(8,128)}) fusion(pred[128,4096]{0,1:T(8,128)(4,1)S(1)} %broadcast_compare_fusion.2, bf16[128,1,8,128]{0,3,2,1:T(8,128)(2,1)S(1)} %get-tuple-element.221, bf16[4096,1,128]{2,0,1:T(8,128)(2,1)} %get-tuple-element.124), kind=kOutput, calls=%fused_computation.33 | convolution fusion | flops 1086323712 | bytes 18616320 | tf_op jit(solution)/shard_map/cond/branch_0_fun/qagd,kad->agqk/dot_general | solution.py:31
  178.1 9.5 %fusion.30 = f32[8,128]{1,0:T(8,128)S(1)} fusion(f32[4096,128,8]{1,0,2:T(8,128)} %get-tuple-element.257, f32[8,128]{1,0:T(8,128)S(1)} %get-tuple-element.254, pred[128,4096]{0,1:T(8,128)(4,1)S(1)} %broadcast_compare_fusion.2), kind=kLoop, calls=%fused_computation.36 | loop fusion | flops 16776192 | bytes 17309696 | tf_op jit(solution)/shard_map/cond/branch_0_fun/reduce_sum | solution.py:43
  187.7 11.2 %conditional.10 = (bf16[1,8,128,128]{3,2,1,0:T(8,128)(2,1)S(1)}) conditional(s32[]{:T(128)} %convert_element_type.90, (s32[4096]{0:T(1024)S(1)}, s32[128]{0:T(128)S(1)}, bf16[4096,1,128]{2,0,1:T(8,128)(2,1)}, bf16[128,1,8,128]{0,3,2,1:T(8,128)(2,1)S(1)}, f32[1,8,128]{2,1,0:T(8,128)S(1)}, ...), branch_computations={%region_13.14_spmd, %region_14.15_spmd} | conditional | flops 2164785152 | bytes 3691016 | solution.py:178
  189.9 9.0 %fusion.44 = bf16[1,8,128,128]{3,2,1,0:T(8,128)(2,1)S(1)} fusion(f32[8,128]{1,0:T(8,128)S(1)} %bitcast.459, pred[128,4096]{0,1:T(8,128)(4,1)S(1)} %broadcast_compare_fusion.3, bf16[4096,1,128]{2,0,1:T(8,128)(2,1)S(1)} %get-tuple-element.131, bf16[4096,1,128]{2,0,1:T(8,128)(2,1)} %get-tuple-element.128, bf16[128,1,8,128]{0,3,2,1:T(8,128)(2,1)S(1)} %get-tuple-element.225), kind=kOutput, calls=%fused_computation.54 | convolution fusion | flops 2164260864 | bytes 3149824 | tf_op jit(solution)/shard_map/cond/branch_0_fun/agqk,kad->agqd/dot_general | solution.py:49
  199.1 19.1 %all-gather = f32[4096,1,8]{0,2,1:T(8,128)S(1)} all-gather(f32[256,1,8]{0,2,1:T(8,128)S(1)} %maximum_bitcast_fusion), channel_id=2, replica_groups=mesh['seq'=16,'tp'=8] {'seq'}, dimensions={0}, use_global_device_ids=true | all-gather | bytes 139264 | tf_op jit(solution)/shard_map/all_gather | solution.py:237
  220.0 28.7 %conditional.12 = (bf16[128,1,8,128]{3,0,2,1:T(8,128)(2,1)S(1)}) conditional(s32[]{:T(128)} %convert_element_type.90, (s32[4096]{0:T(1024)S(1)}, s32[128]{0:T(128)}, bf16[4096,1,128]{2,0,1:T(8,128)(2,1)}, bf16[128,1,8,128]{0,3,2,1:T(8,128)(2,1)}, f32[1,8,128]{2,1,0:T(8,128)}, /*index=5*/bf16[4096,1,128]{2,0,1:T(8,128)(2,1)S(1)}, ...), branch_computations={%region_18.19_spmd, %region_19.20_spmd} | conditional | flops 3247177728 | bytes 44335680 | solution.py:229
  223.1 3.2 broadcast_compare_fusion.5
  226.3 8.2 %fusion.92 = f32[4096,128,8]{1,0,2:T(8,128)} fusion(bf16[128,8,128]{0,2,1:T(8,128)(2,1)S(1)} %bitcast.439, bf16[4096,1,128]{2,0,1:T(8,128)(2,1)S(1)} %get-tuple-element.145), kind=kOutput, calls=%fused_computation.95 | convolution fusion | flops 1073741824 | bytes 18087936 | tf_op jit(solution)/shard_map/cond/branch_0_fun/qagd,kad->agqk/dot_general | solution.py:66
  234.5 14.2 %fusion.89 = bf16[128,1,8,128]{3,0,2,1:T(8,128)(2,1)S(1)} fusion(f32[8,128]{1,0:T(8,128)} %slice_bitcast_fusion.1, f32[4096,128,8]{1,0,2:T(8,128)} %fusion.92, f32[8,128]{1,0:T(8,128)} %bitcast.460, pred[128,4096]{0,1:T(8,128)(4,1)} %broadcast_compare_fusion.5, bf16[4096,1,128]{2,0,1:T(8,128)(2,1)S(1)} %copy-done.2, bf16[128,1,8,128]{0,3,2,1:T(8,128)(2,1)S(1)} %copy-done.6), kind=kOutput, calls=%fused_computation.94 | convolution fusion | flops 2172911616 | bytes 18882560 | tf_op jit(solution)/shard_map/cond/branch_0_fun/agqk,kad->qagd/dot_general | solution.py:70
  249.4 27.6 %conditional.11 = (bf16[128,1,8,128]{3,0,2,1:T(8,128)(2,1)S(1)}) conditional(s32[]{:T(128)} %convert_element_type.86, (s32[4096]{0:T(1024)S(1)}, s32[128]{0:T(128)}, bf16[4096,1,128]{2,0,1:T(8,128)(2,1)}, bf16[128,1,8,128]{0,3,2,1:T(8,128)(2,1)S(1)}, f32[1,8,128]{2,1,0:T(8,128)}, /*index=5*/bf16[4096,1,128]{2,0,1:T(8,128)(2,1)S(1)}, ...), branch_computations={%region_16.17_spmd, %region_17.18_spmd} | conditional | flops 3247177728 | bytes 43303488 | solution.py:229
  252.4 2.6 broadcast_compare_fusion.4
  254.9 8.1 %fusion.69 = f32[4096,128,8]{1,0,2:T(8,128)} fusion(bf16[128,8,128]{0,2,1:T(8,128)(2,1)S(1)} %bitcast.440, bf16[4096,1,128]{2,0,1:T(8,128)(2,1)S(1)} %get-tuple-element.137), kind=kOutput, calls=%fused_computation.74 | convolution fusion | flops 1073741824 | bytes 18087936 | tf_op jit(solution)/shard_map/cond/branch_0_fun/qagd,kad->agqk/dot_general | solution.py:66
  263.0 13.8 %fusion.66 = bf16[128,1,8,128]{3,0,2,1:T(8,128)(2,1)S(1)} fusion(f32[8,128]{1,0:T(8,128)S(1)} %slice_bitcast_fusion, f32[4096,128,8]{1,0,2:T(8,128)} %fusion.69, f32[8,128]{1,0:T(8,128)S(1)} %bitcast.458, pred[128,4096]{0,1:T(8,128)(4,1)S(1)} %broadcast_compare_fusion.4, bf16[4096,1,128]{2,0,1:T(8,128)(2,1)S(1)} %copy-done.3, ...), kind=kOutput, calls=%fused_computation.73 | convolution fusion | flops 2172911616 | bytes 18882560 | tf_op jit(solution)/shard_map/cond/branch_0_fun/agqk,kad->qagd/dot_general | solution.py:70
  279.4 12.0 %fusion.170 = f32[256]{0:T(256)S(1)} fusion(bf16[256,1024]{0,1:T(8,128)(2,1)} %bitcast.447, bf16[1024,8192]{1,0:T(8,128)(2,1)} %param.27, bf16[256,8192]{1,0:T(8,128)(2,1)} %all-gather.12.cloned.1.call-done), kind=kOutput, calls=%fused_computation.143 | convolution fusion | flops 4301258752 | bytes 21496832 | tf_op jit(solution)/shard_map/dot_general | solution.py:280
  291.4 21.0 %psum.7 = f32[256]{0:T(256)} all-reduce(f32[256]{0:T(256)S(1)} %fusion.170), channel_id=1, replica_groups=mesh['seq'=16,'tp'=8] {'tp'}, use_global_device_ids=true, to_apply=%region_25.26 | all-reduce | flops 256 | bytes 2048 | tf_op jit(solution)/shard_map/psum | solution.py:282
  312.3 20.3 %all_gather.37 = f32[4096,8]{0,1:T(8,128)S(1)} all-gather(f32[256,8]{0,1:T(8,128)S(1)} %copy-done.10), channel_id=1, replica_groups=mesh['seq'=16,'tp'=8] {'seq'}, dimensions={0}, use_global_device_ids=true | all-gather | bytes 139264 | tf_op jit(solution)/shard_map/all_gather | solution.py:238
  332.7 58.3 %conditional.13 = (bf16[256,128]{1,0:T(8,128)(2,1)S(1)}, bf16[256,128]{1,0:T(8,128)(2,1)S(1)}) conditional(s32[]{:T(128)} %convert_element_type.95, (s32[256]{0:T(256)S(1)}, s32[4096]{0:T(1024)S(1)}, bf16[4096,1024]{1,0:T(8,128)(2,1)}, bf16[256,128]{1,0:T(8,128)(2,1)S(1)}, f32[1,8,4096]{2,1,0:T(8,128)S(1)}, ...), branch_computations={%region_22.23_spmd, %region_23.24_spmd} | conditional | flops 8674967552 | bytes 138036240 | solution.py:270
  333.3 19.0 %fusion.121 = f32[256,4096,8]{1,0,2:T(8,128)} fusion(bf16[256,128]{1,0:T(8,128)(2,1)S(1)} %get-tuple-element.150, bf16[4096,1024]{1,0:T(8,128)(2,1)} %get-tuple-element.151), kind=kOutput, calls=%fused_computation.120 | convolution fusion | flops 2147483648 | bytes 42008576 | tf_op jit(solution)/shard_map/cond/branch_0_fun/qagd,kad->agqk/dot_general | solution.py:31
  352.3 21.9 %fusion.147 = bf16[256,128]{1,0:T(8,128)(2,1)S(1)} fusion(f32[256,4096,8]{1,0,2:T(8,128)} %fusion.121, f32[8,4096]{1,0:T(8,128)S(1)} %bitcast.453, f32[8,4096]{1,0:T(8,128)S(1)} %bitcast.450, pred[4096,256]{0,1:T(8,128)(4,1)S(1)} %broadcast_compare_fusion.6, bf16[256,128]{1,0:T(8,128)(2,1)S(1)} %get-tuple-element.153, ...), kind=kOutput, calls=%fused_computation.130 | convolution fusion | flops 4345364480 | bytes 51773440 | tf_op jit(solution)/shard_map/cond/branch_0_fun/agqk,qagd->kad/dot_general | solution.py:74
  374.2 16.8 %fusion.154 = bf16[256,128]{1,0:T(8,128)(2,1)S(1)} fusion(f32[256,4096,8]{1,0,2:T(8,128)} %fusion.121, f32[8,4096]{1,0:T(8,128)S(1)} %bitcast.451, pred[4096,256]{0,1:T(8,128)(4,1)S(1)} %broadcast_compare_fusion.6, bf16[4096,1024]{1,0:T(8,128)(2,1)} %get-tuple-element.154), kind=kOutput, calls=%fused_computation.131 | convolution fusion | flops 2181070848 | bytes 43188224 | tf_op jit(solution)/shard_map/cond/branch_0_fun/agqk,qagd->kad/dot_general | solution.py:77
  (89 shorter events, 24.2 us)
Async XLA Ops:
  7.2 81.8 %all-gather.12.cloned.1.call-start = ((), (), s32[]{:S(2)}) async-start(), calls=%async_computation.2 | async-start | bytes 4718592 | tf_op jit(solution)/shard_map/all_gather | solution.py:96
  9.2 112.5 %copy-start.12 = (s32[256]{0:T(256)}, s32[256]{0:T(256)S(1)}, u32[]{:S(2)}) copy-start(s32[256]{0:T(256)S(1)} %get-tuple-element.249) | copy-start | bytes 3076
  14.4 111.8 %copy-start.4 = (bf16[256,1024]{1,0:T(8,128)(2,1)S(1)}, bf16[256,1024]{1,0:T(8,128)(2,1)}, u32[]{:S(2)}) copy-start(bf16[256,1024]{1,0:T(8,128)(2,1)} %param.24) | copy-start | bytes 1572868
  14.5 112.2 %all-gather.8.cloned.1.call-start = ((), (), s32[]{:S(2)}) async-start(), calls=%async_computation | async-start | bytes 1114112 | tf_op jit(solution)/shard_map/all_gather | solution.py:192
  15.2 140.8 %all-gather.10.cloned.1.call-start = ((), (), s32[]{:S(2)}) async-start(), calls=%async_computation.1 | async-start | bytes 1114112 | tf_op jit(solution)/shard_map/all_gather | solution.py:193
  15.9 316.7 %all-gather.14.cloned.1.call-start = ((), (), s32[]{:S(2)}) async-start(), calls=%async_computation.3 | async-start | bytes 8912896 | tf_op jit(solution)/shard_map/all_gather | solution.py:245
  16.5 316.1 %all-gather.16.cloned.1.call-start = ((), (), s32[]{:S(2)}) async-start(), calls=%async_computation.4 | async-start | bytes 8912896 | tf_op jit(solution)/shard_map/all_gather | solution.py:246
  122.3 33.7 %copy-start.17 = (s32[128]{0:T(128)}, s32[128]{0:T(128)S(1)}, u32[]{:S(2)}) copy-start(s32[128]{0:T(128)S(1)} %get-tuple-element.260) | copy-start | bytes 1540
  122.3 65.4 %copy-start.18 = (s32[128]{0:T(128)}, s32[128]{0:T(128)S(1)}, u32[]{:S(2)}) copy-start(s32[128]{0:T(128)S(1)} %get-tuple-element.262) | copy-start | bytes 1540
  126.6 61.1 %copy-start.5 = (bf16[128,1024]{0,1:T(8,128)(2,1)}, bf16[128,1024]{0,1:T(8,128)(2,1)S(1)}, u32[]{:S(2)}) copy-start(bf16[128,1024]{0,1:T(8,128)(2,1)S(1)} %copy.77) | copy-start | bytes 786436
  146.6 52.5 %copy-start.14 = (f32[1,8,128]{2,1,0:T(8,128)}, f32[1,8,128]{2,1,0:T(8,128)S(1)}, u32[]{:S(2)}) copy-start(f32[1,8,128]{2,1,0:T(8,128)S(1)} %add.24) | copy-start | bytes 12292
  167.5 20.2 %copy-start.1 = (bf16[4096,128]{1,0:T(8,128)(2,1)S(1)}, bf16[4096,128]{1,0:T(8,128)(2,1)}, u32[]{:S(2)}) copy-start(bf16[4096,128]{1,0:T(8,128)(2,1)} %all-gather.10.cloned.1.call-done) | copy-start | bytes 3145732
  187.7 31.4 %copy-start = (bf16[256,1024]{1,0:T(8,128)(2,1)S(1)}, bf16[256,1024]{1,0:T(8,128)(2,1)}, u32[]{:S(2)}) copy-start(bf16[256,1024]{1,0:T(8,128)(2,1)} %fusion.171) | copy-start | bytes 1572868
  187.7 30.5 %copy-start.16 = (f32[1,8,128]{2,1,0:T(8,128)}, f32[1,8,128]{2,1,0:T(8,128)S(1)}, u32[]{:S(2)}) copy-start(f32[1,8,128]{2,1,0:T(8,128)S(1)} %add.27) | copy-start | bytes 12292
  219.4 0.6 copy-start.9
  220.5 14.1 %copy-start.2 = (bf16[4096,1,128]{2,0,1:T(8,128)(2,1)S(1)}, bf16[4096,1,128]{2,0,1:T(8,128)(2,1)}, u32[]{:S(2)}) copy-start(bf16[4096,1,128]{2,0,1:T(8,128)(2,1)} %get-tuple-element.142) | copy-start | bytes 3145732 | tf_op jit(solution)/shard_map/cond
  220.5 14.1 %copy-start.6 = (bf16[128,1,8,128]{0,3,2,1:T(8,128)(2,1)S(1)}, bf16[128,1,8,128]{0,3,2,1:T(8,128)(2,1)}, u32[]{:S(2)}) copy-start(bf16[128,1,8,128]{0,3,2,1:T(8,128)(2,1)} %get-tuple-element.239) | copy-start | bytes 786436 | tf_op jit(solution)/shard_map/cond
  248.7 0.7 copy-start.8
  249.6 13.4 %copy-start.3 = (bf16[4096,1,128]{2,0,1:T(8,128)(2,1)S(1)}, bf16[4096,1,128]{2,0,1:T(8,128)(2,1)}, u32[]{:S(2)}) copy-start(bf16[4096,1,128]{2,0,1:T(8,128)(2,1)} %get-tuple-element.134) | copy-start | bytes 3145732 | tf_op jit(solution)/shard_map/cond
  249.6 13.4 %copy-start.15 = (f32[1,8,128]{2,1,0:T(8,128)S(1)}, f32[1,8,128]{2,1,0:T(8,128)}, u32[]{:S(2)}) copy-start(f32[1,8,128]{2,1,0:T(8,128)} %get-tuple-element.136) | copy-start | bytes 12292 | tf_op jit(solution)/shard_map/cond
  277.1 35.3 %copy-start.10 = (f32[256,8]{0,1:T(8,128)S(1)}, f32[256,8]{0,1:T(8,128)}, u32[]{:S(2)}) copy-start(f32[256,8]{0,1:T(8,128)} %copy-done.9) | copy-start | bytes 24580
  277.1 55.6 %copy-start.7 = (bf16[256,128]{1,0:T(8,128)(2,1)S(1)}, bf16[256,128]{1,0:T(8,128)(2,1)}, u32[]{:S(2)}) copy-start(bf16[256,128]{1,0:T(8,128)(2,1)} %param.25) | copy-start | bytes 196612
  277.1 55.5 %copy-start.11 = (bf16[256,128]{1,0:T(8,128)(2,1)S(1)}, bf16[256,128]{1,0:T(8,128)(2,1)}, u32[]{:S(2)}) copy-start(bf16[256,128]{1,0:T(8,128)(2,1)} %param.26) | copy-start | bytes 196612
  277.1 55.5 %copy-start.13 = (s32[256]{0:T(256)S(1)}, s32[256]{0:T(256)}, u32[]{:S(2)}) copy-start(s32[256]{0:T(256)} %copy-done.12) | copy-start | bytes 3076
  391.0 0.6 copy-start.19
  391.0 0.6 copy-start.20
Sparse Core Ops, SparseCore 0:
  14.6 74.3 all-gather.11
  90.7 30.9 all-gather.7
  123.4 32.5 all-gather.9
  157.6 52.7 all-gather.13
  211.9 52.9 all-gather.15
where the time goes:
time: 404 us; the launch traced here: 398 us
  matrix products  161 us (40%)
  waiting for transfers between devices  83.8 us (21%)
  blocking collectives  79.9 us (20%)
  other arithmetic  39.1 us (10%)
  between operations  18.2 us (5%)
  local copies, waits for them, and re-layouts  13.8 us (3%)
    all_gather x1, waiting for transfers between devices, body(): picked_full = lax.all_gather(picked, 'tp', axis=1, tiled=True)  72.4 us
    dot_general x3, matrix products, masked_scores(): jnp.einsum('qagd,kad->agqk', queries, key_block, preferred_element_type=j...  35.7 us
    dot_general x2, matrix products, backward_terms(): jnp.einsum('agqk,kad->qagd', grad_scores, key_block, preferred_element_ty...  28 us
    dot_general x1, matrix products, backward_terms(): jnp.einsum('agqk,qagd->kad', grad_scores, queries, preferred_element_type...  21.9 us
    psum x1, blocking collectives, body(): grad_router = lax.psum(router_term, 'tp')  21 us
    all_gather x1, blocking collectives, body(): lax.all_gather(deltas_flat, 'seq', axis=0, tiled=True)  20.3 us
    all_gather x1, blocking collectives, body(): lax.all_gather(places, 'seq', axis=0, tiled=True)  19.6 us
    all_gather x1, blocking collectives, body(): lax.all_gather(logs_flat, 'seq', axis=0, tiled=True)  19.1 us
  transfers between devices with their start and end apart: 5, of which 2 were waited for; matrix products, arithmetic and copies ran while one was open for 37% of the time, Pallas kernels for 0%

commit v1 on v0

v1 whole, which is shorter than its diff:
```python
import math

import jax
import jax.numpy as jnp
from jax import lax
from jax.experimental import pallas as pl
from jax.experimental.pallas import tpu as pltpu
from jax.sharding import PartitionSpec as P

F32 = jnp.float32
BF = jnp.bfloat16
MESH = pl.DeviceIdType.MESH
NN = ((1,), (0,))
NT = ((1,), (1,))
TN = ((0,), (0,))

HD = 128
GROUP = 8
SEQ = 16
TP = 8
CHIPS = 8
ROWS = 256
HALF = 128
LANES = 1024
WIDE = 1024
FACTOR = 1.0 / math.sqrt(HD)
SCALE = FACTOR * math.log2(math.e)
FLOOR = -1e30


def dot(a, b, dims):
    return lax.dot_general(a, b, (dims, ((), ())), preferred_element_type=F32)


def loop(count, step):
    def run(i, carry):
        step(i)
        return carry

    lax.fori_loop(0, count, run, 0)


def kernel(
    go_hbm,
    w_hbm,
    sel_ref,
    router_ref,
    q_ref,
    k_ref,
    v_ref,
    dq_ref,
    dk_ref,
    dv_ref,
    gr_ref,
    probs,
    w_ref,
    picked,
    kv,
    acc,
    out_part,
    in_part,
    q_t,
    q_s,
    top,
    o_t,
    g_t,
    do_t,
    do_s,
    delta,
    dq_t,
    router_part,
    local_sem,
    kv_send,
    kv_recv,
    side_send,
    pick_send,
    pick_recv,
    part_send,
    part_recv,
    router_send,
    router_recv,
):
    s = lax.axis_index("seq")
    t = lax.axis_index("tp")
    chip = s // 2
    core = s % 2
    z = t // 2
    h = t % 2
    sibling = s + 1 - 2 * core
    z_up = ((z + 1) % 4) * 2 + h
    z_down = ((z + 3) % 4) * 2 + h
    z_far = ((z + 2) % 4) * 2 + h
    x_far = z * 2 + 1 - h
    other = 1 - 2 * h

    go_copies = []
    for p in range(4):
        go_copies.append(
            pltpu.make_async_copy(
                go_hbm.at[pl.ds(p * 512, 512), :],
                probs.at[p // 2, :, pl.ds((p % 2) * WIDE, WIDE)],
                local_sem.at[p],
            )
        )
    for copy in go_copies:
        copy.start()
    w_copy = pltpu.make_async_copy(w_hbm, w_ref, local_sem.at[4])
    w_copy.start()

    barrier = pltpu.get_barrier_semaphore()
    for step in range(1, SEQ):
        pl.semaphore_signal(
            barrier, inc=1, device_id=((s + step) % SEQ, t), device_id_type=MESH
        )
    for step in range(1, TP):
        pl.semaphore_signal(
            barrier, inc=1, device_id=(s, (t + step) % TP), device_id_type=MESH
        )
    kv[s, 0] = k_ref[...]
    kv[s, 1] = v_ref[...]
    pl.semaphore_wait(barrier, SEQ - 1 + TP - 1)

    def kv_copy(step):
        return pltpu.make_async_remote_copy(
            src_ref=kv.at[s],
            dst_ref=kv.at[s],
            send_sem=kv_send.at[step],
            recv_sem=kv_recv.at[s],
            device_id=(((chip + step) % CHIPS) * 2 + core, t),
            device_id_type=MESH,
        )

    def side_copy(step):
        block = ((chip + CHIPS - step) % CHIPS) * 2 + core
        return pltpu.make_async_remote_copy(
            src_ref=kv.at[block],
            dst_ref=kv.at[block],
            send_sem=side_send.at[step],
            recv_sem=kv_recv.at[block],
            device_id=(sibling, t),
            device_id_type=MESH,
        )

    def kv_arrived(block):
        pltpu.make_async_remote_copy(
            src_ref=kv.at[block],
            dst_ref=kv.at[block],
            send_sem=kv_send.at[0],
            recv_sem=kv_recv.at[block],
            device_id=(sibling, t),
            device_id_type=MESH,
        ).wait_recv()

    side_copy(0).start()
    for step in range(1, CHIPS):
        kv_copy(step).start()

    def pick_copy(c, n, slot, to, rows=None):
        src = picked.at[c, slot]
        if rows is not None:
            src = picked.at[c, slot, pl.ds(rows, HALF // 2), :]
        return pltpu.make_async_remote_copy(
            src_ref=src,
            dst_ref=src,
            send_sem=pick_send.at[c, n],
            recv_sem=pick_recv.at[c, n],
            device_id=(s, to),
            device_id_type=MESH,
        )

    def own_sends(c):
        return [
            pick_copy(c, 0, t, z_up),
            pick_copy(c, 1, t, z_down),
            pick_copy(c, 2, t, x_far),
        ]

    def near_sends(c):
        return [
            pick_copy(c, 3, z_down, z_up, 0),
            pick_copy(c, 4, z_up, z_down, HALF // 2),
            pick_copy(c, 5, x_far, z_up),
            pick_copy(c, 6, x_far, z_down),
        ]

    def far_sends(c):
        return [pick_copy(c, 7, z_far, x_far)]

    def near_arrivals(c):
        return [
            pick_copy(c, 0, z_down, z_up),
            pick_copy(c, 1, z_up, z_down),
            pick_copy(c, 2, x_far, x_far),
        ]

    def half_arrivals(c):
        return [
            pick_copy(c, 3, z_far, z_up, 0),
            pick_copy(c, 4, z_far, z_down, HALF // 2),
        ]

    def last_arrivals(c):
        return [
            pick_copy(c, 5, z_down + other, z_up),
            pick_copy(c, 6, z_up + other, z_down),
            pick_copy(c, 7, z_far + other, x_far),
        ]

    def start_all(copies):
        for copy in copies:
            copy.start()

    def arrive_all(copies):
        for copy in copies:
            copy.wait_recv()

    for copy in go_copies:
        copy.wait()
    sel_wide = jnp.transpose(jnp.broadcast_to(sel_ref[...], (HALF, ROWS)))
    for c in range(2):
        sel_half = sel_wide[c * HALF : (c + 1) * HALF]
        total = jnp.zeros((HALF, WIDE), F32)
        for p in range(4):
            pieces = []
            for b in range(4):
                token = lax.broadcasted_iota(jnp.int32, (HALF, HALF), 1) + (p * 512 + b * 128)
                pieces.append(jnp.where(token == sel_half, 1.0, 0.0).astype(BF))
            chosen = jnp.concatenate(pieces, axis=1)
            total += dot(chosen, probs[p // 2, :, (p % 2) * WIDE : (p % 2 + 1) * WIDE], NN)
        picked[c, t] = total.astype(BF)
        if c == 0:
            start_all(own_sends(0))

    for c in range(2):
        for n in range(GROUP):
            block = q_ref[c * HALF : (c + 1) * HALF, n * HD : (n + 1) * HD]
            at = c * LANES + n * HALF
            q_s[at : at + HALF, :] = block
            q_t[:, at : at + HALF] = jnp.transpose(block)

    def rank_of(c):
        return s * ROWS + c * HALF

    def hidden(k, c):
        key_at = lax.broadcasted_iota(jnp.int32, (512, LANES), 0) + k * 512
        row_at = (lax.broadcasted_iota(jnp.int32, (512, LANES), 1) % HALF) + rank_of(c)
        return key_at > row_at

    def keys_of(k):
        return jnp.concatenate([kv[2 * k, 0], kv[2 * k + 1, 0]], axis=0)

    def values_of(k):
        return jnp.concatenate([kv[2 * k, 1], kv[2 * k + 1, 1]], axis=0)

    top[...] = jnp.full_like(top, FLOOR)

    def first_pass(k, masked):
        keys = keys_of(k)
        for c in range(2):
            lanes = pl.ds(c * LANES, LANES)
            scores = dot(keys, q_t[:, lanes], NN)
            if masked:
                scores = jnp.where(hidden(k, c), FLOOR, scores)
            top[:, lanes] = jnp.maximum(
                top[:, lanes], jnp.max(scores.reshape(64, 8, LANES), axis=0)
            )

    def near_step(c):
        arrive_all(near_arrivals(c))
        start_all(near_sends(c))

    def far_step(c):
        arrive_all(half_arrivals(c))
        start_all(far_sends(c))

    def first_step(d):
        k = (chip + CHIPS - d) % CHIPS

        @pl.when(d > 0)
        def _():
            kv_arrived(k * 2 + core)
            side_copy(d).start()

        kv_arrived(k * 2 + 1 - core)

        @pl.when(d == 0)
        def _():
            first_pass(k, True)

        @pl.when((d > 0) & (k < chip))
        def _():
            first_pass(k, False)

    loop(CHIPS, first_step)
    near_step(0)

    peak = jnp.max(top[...], axis=0, keepdims=True) * SCALE
    top[...] = jnp.broadcast_to(peak, top.shape)
    o_t[...] = jnp.zeros_like(o_t)

    def second_pass(k, masked):
        keys = keys_of(k)
        values_t = jnp.concatenate(
            [jnp.transpose(values_of(k)), jnp.ones((16, 512), BF)], axis=0
        )
        for c in range(2):
            lanes = pl.ds(c * LANES, LANES)
            scores = dot(keys, q_t[:, lanes], NN) * SCALE - top[0:1, lanes]
            if masked:
                scores = jnp.where(hidden(k, c), FLOOR, scores)
            weights = jnp.exp2(scores).astype(BF)
            probs[k, :, lanes] = weights
            o_t[:, lanes] += dot(values_t, weights, NN)

    def second_step(d):
        k = chip - d

        @pl.when(d == 0)
        def _():
            second_pass(k, True)

        @pl.when((d > 0) & (k >= 0))
        def _():
            second_pass(k, False)

        @pl.when(d == 3)
        def _():
            far_step(0)
            start_all(own_sends(1))

    loop(CHIPS, second_step)

    def project(c, slots, fresh):
        total = None
        for slot in slots:
            columns = pl.ds(pl.multiple_of(slot * WIDE, WIDE), WIDE)
            term = dot(w_ref[:, columns], picked[c, slot], NT)
            total = term if total is None else total + term
        if fresh:
            g_t[...] = total
        else:
            g_t[...] += total

    def near_slots():
        return [t, z_down, z_up, x_far]

    def far_slots():
        return [z_far, z_down + other, z_up + other, z_far + other]

    router_part[t] = jnp.zeros((8, HALF), F32)

    def cotangents(c):
        router_row = router_ref[0:1, c * HALF : (c + 1) * HALF]
        router_sum = jnp.zeros((1, HALF), F32)
        for n in range(GROUP):
            at = c * LANES + n * HALF
            g = g_t[n * HD : (n + 1) * HD, :]
            inverse = 1.0 / o_t[HD : HD + 1, at : at + HALF]
            share = jnp.sum(g * o_t[0:HD, at : at + HALF], axis=0, keepdims=True) * inverse
            router_sum += share
            level = router_row * inverse
            delta[0:1, n * HALF : (n + 1) * HALF] = share * level
            scaled = g * level
            do_t[:, n * HALF : (n + 1) * HALF] = scaled.astype(BF)
            do_s[n * HALF : (n + 1) * HALF, :] = jnp.transpose(scaled).astype(BF)
        router_part[t, c : c + 1, :] = router_sum

    def part_copy(j, source):
        return pltpu.make_async_remote_copy(
            src_ref=out_part.at[j],
            dst_ref=in_part.at[source],
            send_sem=part_send.at[j],
            recv_sem=part_recv.at[source],
            device_id=(j, t),
            device_id_type=MESH,
        )

    def backward_step(c, k):
        lanes = pl.ds(c * LANES, LANES)
        keys = keys_of(k)
        weights = probs[k, :, lanes]
        grad_probs = dot(values_of(k), do_t[...], NN) - delta[0:1, :]
        grad_scores = (weights.astype(F32) * grad_probs).astype(BF)
        d_values = dot(weights, do_s[...], NN)
        d_keys = dot(grad_scores, q_s[lanes, :], NN)
        d_queries = dot(keys, grad_scores, TN)
        dq_t[...] += d_queries
        if c == 0:
            acc[k, 0] = d_keys
            acc[k, 1] = d_values
        else:
            d_keys = acc[k, 0] + d_keys
            d_values = acc[k, 1] + d_values
            acc[k, 0] = d_keys
            acc[k, 1] = d_values
            for u in range(2):
                j = 2 * k + u
                out_part[j, 0] = d_keys[u * ROWS : (u + 1) * ROWS].astype(BF)
                out_part[j, 1] = d_values[u * ROWS : (u + 1) * ROWS].astype(BF)

                @pl.when(j < s)
                def _():
                    part_copy(j, s).start()

    def store_queries(c):
        for n in range(GROUP):
            block = jnp.transpose(dq_t[:, n * HALF : (n + 1) * HALF]) * FACTOR
            dq_ref[c * HALF : (c + 1) * HALF, n * HD : (n + 1) * HD] = block.astype(BF)

    def router_copy(step, slot):
        return pltpu.make_async_remote_copy(
            src_ref=router_part.at[slot],
            dst_ref=router_part.at[slot],
            send_sem=router_send.at[step],
            recv_sem=router_recv.at[slot],
            device_id=(s, (t + step) % TP),
            device_id_type=MESH,
        )

    w_copy.wait()
    project(0, near_slots(), True)
    arrive_all(last_arrivals(0))
    project(0, far_slots(), False)
    cotangents(0)
    dq_t[...] = jnp.zeros_like(dq_t)

    def early_step(k):
        @pl.when(k <= chip)
        def _():
            backward_step(0, k)

        @pl.when(k == 1)
        def _():
            near_step(1)

        @pl.when(k == 4)
        def _():
            far_step(1)

    loop(CHIPS, early_step)
    store_queries(0)

    project(1, near_slots(), True)
    arrive_all(last_arrivals(1))
    project(1, far_slots(), False)
    cotangents(1)
    for step in range(1, TP):
        router_copy(step, t).start()
    dq_t[...] = jnp.zeros_like(dq_t)
    loop(chip + 1, lambda k: backward_step(1, k))
    store_queries(1)

    router_total = router_part[t]
    for step in range(1, TP):
        slot = (t + step) % TP
        router_copy(step, slot).wait_recv()
        router_total += router_part[slot]
    gr_ref[...] = router_total

    own = pl.ds(pl.multiple_of(core * ROWS, ROWS), ROWS)
    dk_sum = acc[chip, 0, own, :]
    dv_sum = acc[chip, 1, own, :]
    acc[0, 0, 0:ROWS, :] = dk_sum
    acc[0, 1, 0:ROWS, :] = dv_sum

    def collect(n):
        source = SEQ - 1 - n

        @pl.when(source > s)
        def _():
            part_copy(s, source).wait_recv()
            acc[0, 0, 0:ROWS, :] += in_part[source, 0].astype(F32)
            acc[0, 1, 0:ROWS, :] += in_part[source, 1].astype(F32)

    loop(SEQ, collect)
    dk_ref[...] = (acc[0, 0, 0:ROWS, :] * FACTOR).astype(BF)
    dv_ref[...] = acc[0, 1, 0:ROWS, :].astype(BF)

    side_copy(0).wait_send()
    for step in range(1, CHIPS):
        kv_copy(step).wait_send()
        side_copy(step).wait_send()
    for c in range(2):
        for copy in own_sends(c) + near_sends(c) + far_sends(c):
            copy.wait_send()
    for step in range(1, TP):
        router_copy(step, t).wait_send()

    def sent(j):
        @pl.when(j < s)
        def _():
            part_copy(j, s).wait_send()

    loop(SEQ, sent)


def body(grad_out, select, router, query, key_rows, value_rows, out_weight):
    vmem = pl.BlockSpec(memory_space=pltpu.VMEM)
    hbm = pl.BlockSpec(memory_space=pl.ANY)
    dma = pltpu.SemaphoreType.DMA
    dq, dk, dv, gr = pl.pallas_call(
        kernel,
        out_shape=(
            jax.ShapeDtypeStruct((ROWS, WIDE), BF),
            jax.ShapeDtypeStruct((ROWS, HD), BF),
            jax.ShapeDtypeStruct((ROWS, HD), BF),
            jax.ShapeDtypeStruct((8, HALF), F32),
        ),
        in_specs=[hbm, hbm] + [vmem] * 5,
        out_specs=(vmem,) * 4,
        scratch_shapes=[
            pltpu.VMEM((CHIPS, 512, 2 * LANES), BF),
            pltpu.VMEM((WIDE, TP * WIDE), BF),
            pltpu.VMEM((2, TP, HALF, WIDE), BF),
            pltpu.VMEM((SEQ, 2, ROWS, HD), BF),
            pltpu.VMEM((CHIPS, 2, 512, HD), F32),
            pltpu.VMEM((SEQ, 2, ROWS, HD), BF),
            pltpu.VMEM((SEQ, 2, ROWS, HD), BF),
            pltpu.VMEM((HD, 2 * LANES), BF),
            pltpu.VMEM((2 * LANES, HD), BF),
            pltpu.VMEM((8, 2 * LANES), F32),
            pltpu.VMEM((HD + 16, 2 * LANES), F32),
            pltpu.VMEM((WIDE, HALF), F32),
            pltpu.VMEM((HD, LANES), BF),
            pltpu.VMEM((LANES, HD), BF),
            pltpu.VMEM((8, LANES), F32),
            pltpu.VMEM((HD, LANES), F32),
            pltpu.VMEM((TP, 8, HALF), F32),
            dma((5,)),
            dma((CHIPS,)),
            dma((SEQ,)),
            dma((CHIPS,)),
            dma((2, 8)),
            dma((2, 8)),
            dma((SEQ,)),
            dma((SEQ,)),
            dma((TP,)),
            dma((TP,)),
        ],
        compiler_params=pltpu.CompilerParams(
            collective_id=0, has_side_effects=True, vmem_limit_bytes=62 << 20
        ),
    )(
        grad_out,
        out_weight,
        select.reshape(1, ROWS),
        router.reshape(1, ROWS),
        query,
        key_rows,
        value_rows,
    )
    return dq, dk, dv, gr[0:2].reshape(ROWS)


def solution(mesh):
    return jax.shard_map(
        body,
        mesh=mesh,
        in_specs=(
            P("seq", "tp"),
            P("seq"),
            P("seq"),
            P("seq", "tp"),
            P("seq", "tp"),
            P("seq", "tp"),
            P("tp", None),
        ),
        out_specs=(P("seq", "tp"), P("seq", "tp"), P("seq", "tp"), P("seq")),
        check_vma=False,
    )
```

time: 404 us -> 102 us (0.25)
  the two profiles are of different devices: /device:TPU:1 before, /device:TPU:19 now
where the time goes in v1:
time: 102 us
  Pallas kernels  95.4 us (94%)
  local copies, waits for them, and re-layouts  6.06 us (6%)
    pallas_call x1, Pallas kernels, body(): pl.pallas_call(kernel, out_shape=(jax.ShapeDtypeStruct((ROWS, WIDE), BF),...  95.4 us
    unnamed x3, local copies, waits for them, and re-layouts  4.81 us

profile of v1, /device:TPU:19, one launch (start us, length us, event | category | flops | bytes accessed | tf_op | source)
XLA Modules:
  0.0 102.1 jit_solution(14051224973845294442)
XLA Ops:
  0.6 95.4 %shard_map.102 = (bf16[256,1024]{1,0:T(8,128)(2,1)}, bf16[256,128]{1,0:T(8,128)(2,1)}, bf16[256,128]{1,0:T(8,128)(2,1)}, f32[8,128]{1,0:T(8,128)}) custom-call(bf16[2048,1024]{1,0:T(8,128)(2,1)} %go_hbm.1, bf16[1024,8192]{1,0:T(8,128)(2,1)} %w_hbm.1, s32[1,256]{1,0:T(1,128)} %bitcast.4, f32[1,256]{1,0:T(1,128)} %bitcast.5, bf16[256,1024]{1,0:T(8,128)(2,1)} %q_ref.1, ...), custom_call_target="tpu_custom_call" | custom-call | tf_op jit(solution)/shard_map/pallas_call | solution.py:501
  96.1 1.2 %slice_bitcast_fusion = f32[256]{0:T(256)} fusion(f32[8,128]{1,0:T(8,128)} %get-tuple-element.11), kind=kLoop, calls=%fused_computation | loop fusion | bytes 2048 | tf_op jit(solution)/shard_map/reshape | solution.py:552
  97.3 1.9 %copy.14 = bf16[256,1024]{1,0:T(8,128)(2,1)} copy(bf16[256,1024]{1,0:T(8,128)(2,1)} %get-tuple-element.16) | data formatting | bytes 1048576
  99.2 1.5 %copy.15 = bf16[256,128]{1,0:T(8,128)(2,1)} copy(bf16[256,128]{1,0:T(8,128)(2,1)} %get-tuple-element.17) | data formatting | bytes 131072
  100.6 1.5 %copy.16 = bf16[256,128]{1,0:T(8,128)(2,1)} copy(bf16[256,128]{1,0:T(8,128)(2,1)} %get-tuple-element.18) | data formatting | bytes 131072

commit v2 on v1

v2 whole, which is shorter than its diff:
```python
import math

import jax
import jax.numpy as jnp
from jax import lax
from jax.experimental import pallas as pl
from jax.experimental.pallas import tpu as pltpu
from jax.sharding import PartitionSpec as P

F32 = jnp.float32
BF = jnp.bfloat16
MESH = pl.DeviceIdType.MESH
NN = ((1,), (0,))
NT = ((1,), (1,))
TN = ((0,), (0,))

HD = 128
GROUP = 8
SEQ = 16
TP = 8
CHIPS = 8
ROWS = 256
HALF = 128
LANES = 2048
WIDE = 1024
FACTOR = 1.0 / math.sqrt(HD)
SCALE = FACTOR * math.log2(math.e)
FLOOR = -1e30


def dot(a, b, dims):
    return lax.dot_general(a, b, (dims, ((), ())), preferred_element_type=F32)


def loop(count, step):
    def run(i, carry):
        step(i)
        return carry

    lax.fori_loop(0, count, run, 0)


def loop_from(first, last, step):
    def run(i, carry):
        step(i)
        return carry

    lax.fori_loop(first, last, run, 0)


def kernel(
    go_hbm,
    w_hbm,
    sel_ref,
    router_ref,
    q_ref,
    k_ref,
    v_ref,
    dq_ref,
    dk_ref,
    dv_ref,
    gr_ref,
    probs,
    w_ref,
    picked,
    keys,
    values,
    acc,
    out_side,
    in_side,
    out_part,
    in_part,
    q_t,
    q_s,
    top,
    o_t,
    g_t,
    do_t,
    do_s,
    delta,
    dq_t,
    router_part,
    local_sem,
    kv_send,
    kv_recv,
    side_send,
    pick_send,
    pick_recv,
    fold_send,
    fold_recv,
    part_send,
    part_recv,
    router_send,
    router_recv,
):
    s = lax.axis_index("seq")
    t = lax.axis_index("tp")
    chip = s // 2
    core = s % 2
    y = chip // 2
    xl = chip % 2
    z = t // 2
    h = t % 2
    sibling = s + 1 - 2 * core
    z_up = ((z + 1) % 4) * 2 + h
    z_down = ((z + 3) % 4) * 2 + h
    z_far = ((z + 2) % 4) * 2 + h
    x_far = z * 2 + 1 - h
    other = 1 - 2 * h

    def remote(src, dst, send, recv, to):
        return pltpu.make_async_remote_copy(
            src_ref=src,
            dst_ref=dst,
            send_sem=send,
            recv_sem=recv,
            device_id=to,
            device_id_type=MESH,
        )

    go_copies = []
    for p in range(4):
        go_copies.append(
            pltpu.make_async_copy(
                go_hbm.at[pl.ds(p * 512, 512), :],
                probs.at[p // 2, :, pl.ds((p % 2) * WIDE, WIDE)],
                local_sem.at[p],
            )
        )
    for copy in go_copies:
        copy.start()
    w_copy = pltpu.make_async_copy(w_hbm, w_ref, local_sem.at[4])
    w_copy.start()

    barrier = pltpu.get_barrier_semaphore()
    pl.semaphore_signal(barrier, inc=1, device_id=(sibling, t), device_id_type=MESH)
    for step in range(1, CHIPS):
        pl.semaphore_signal(
            barrier,
            inc=1,
            device_id=(((chip + step) % CHIPS) * 2 + core, t),
            device_id_type=MESH,
        )
    for step in range(1, TP):
        pl.semaphore_signal(
            barrier, inc=1, device_id=(s, (t + step) % TP), device_id_type=MESH
        )
    mine = pl.ds(pl.multiple_of(core * ROWS, ROWS), ROWS)
    theirs = pl.ds(pl.multiple_of((1 - core) * ROWS, ROWS), ROWS)
    keys[chip, mine, :] = k_ref[...]
    values[chip, mine, :] = v_ref[...]

    def choose(c):
        sel_half = jnp.transpose(
            jnp.broadcast_to(sel_ref[0:1, c * HALF : (c + 1) * HALF], (HALF, HALF))
        )
        total = jnp.zeros((HALF, WIDE), F32)
        for p in range(4):
            pieces = []
            for b in range(4):
                token = lax.broadcasted_iota(jnp.int32, (HALF, HALF), 1) + (p * 512 + b * 128)
                pieces.append(jnp.where(token == sel_half, 1.0, 0.0).astype(BF))
            chosen = jnp.concatenate(pieces, axis=1)
            total += dot(chosen, probs[p // 2, :, (p % 2) * WIDE : (p % 2 + 1) * WIDE], NN)
        picked[t, c * HALF : (c + 1) * HALF, :] = total.astype(BF)

    for copy in go_copies:
        copy.wait()
    choose(0)
    pl.semaphore_wait(barrier, CHIPS + TP - 1)

    def block_of(i, block):
        rows = pl.ds(pl.multiple_of((block % 2) * ROWS, ROWS), ROWS)
        return (keys, values)[i].at[block // 2, rows, :]

    def kv_copy(i, n, block, to):
        part = block_of(i, block)
        return remote(part, part, kv_send.at[i, n], kv_recv.at[i, block], (to, t))

    def later_chips(i, act):
        for step in range(1, CHIPS):

            @pl.when(chip + step < CHIPS)
            def _(step=step):
                act(kv_copy(i, step, s, (chip + step) * 2 + core))

    def side_copy(i, d):
        block = (chip - d) * 2 + core
        part = block_of(i, block)
        return remote(part, part, side_send.at[i, d], kv_recv.at[i, block], (sibling, t))

    def kv_ahead(i, d):
        @pl.when(d <= chip)
        def _():
            kv_copy(i, 0, (chip - d) * 2 + core, sibling).wait_recv()
            side_copy(i, d).start()

    def kv_arrived(i, d):
        kv_copy(i, 0, (chip - d) * 2 + 1 - core, sibling).wait_recv()

    def start_all(copies):
        for copy in copies:
            copy.start()

    def arrive_all(copies):
        for copy in copies:
            copy.wait_recv()

    side_copy(0, 0).start()
    later_chips(0, lambda copy: copy.start())
    side_copy(1, 0).start()

    def pick_copy(c, n, slot, to, at=0, rows=HALF):
        src = picked.at[slot, pl.ds(c * HALF + at, rows), :]
        return remote(src, src, pick_send.at[c, n], pick_recv.at[c, n], (s, to))

    quarter = HALF // 2

    def own_sends(c):
        return [
            pick_copy(c, 2, t, x_far),
            pick_copy(c, 0, t, z_up),
            pick_copy(c, 1, t, z_down),
        ]

    def half_sends(c):
        return [
            pick_copy(c, 3, z_down, z_up, 0, quarter),
            pick_copy(c, 4, z_up, z_down, quarter, quarter),
        ]

    def cross_sends(c):
        return [pick_copy(c, 5, x_far, z_up), pick_copy(c, 6, x_far, z_down)]

    def far_sends(c):
        return [pick_copy(c, 7, z_far, x_far)]

    def near_arrivals(c):
        return [pick_copy(c, 0, z_down, z_up), pick_copy(c, 1, z_up, z_down)]

    def x_arrivals(c):
        return [pick_copy(c, 2, x_far, x_far)]

    def half_arrivals(c):
        return [
            pick_copy(c, 3, z_far, z_up, 0, quarter),
            pick_copy(c, 4, z_far, z_down, quarter, quarter),
        ]

    def cross_arrivals(c):
        return [
            pick_copy(c, 5, z_down + other, z_up),
            pick_copy(c, 6, z_up + other, z_down),
        ]

    def far_arrivals(c):
        return [pick_copy(c, 7, z_far + other, x_far)]

    start_all(own_sends(0))
    choose(1)
    start_all(own_sends(1))
    later_chips(1, lambda copy: copy.start())

    for n in range(GROUP):
        block = q_ref[:, n * HD : (n + 1) * HD]
        q_s[n * ROWS : (n + 1) * ROWS, :] = block
        q_t[:, n * ROWS : (n + 1) * ROWS] = jnp.transpose(block)

    def hidden(k):
        key_at = lax.broadcasted_iota(jnp.int32, (512, LANES), 0) + k * 512
        row_at = (lax.broadcasted_iota(jnp.int32, (512, LANES), 1) % ROWS) + s * ROWS
        return key_at > row_at

    top[...] = jnp.full_like(top, FLOOR)

    def first_pass(k, masked):
        scores = dot(keys[k], q_t[...], NN)
        if masked:
            scores = jnp.where(hidden(k), FLOOR, scores)
        top[...] = jnp.maximum(top[...], jnp.max(scores.reshape(64, 8, LANES), axis=0))

    def first_step(d):
        kv_ahead(0, d + 1)

        @pl.when(d <= chip)
        def _():
            kv_arrived(0, d)
            first_pass(chip - d, False)

        @pl.when(d == 5)
        def _():
            arrive_all(near_arrivals(0))
            start_all(half_sends(0))

    kv_arrived(0, 0)
    kv_ahead(0, 1)
    first_pass(chip, True)
    loop_from(1, CHIPS, first_step)
    kv_ahead(1, 1)

    peak = jnp.max(top[...], axis=0, keepdims=True) * SCALE
    top[...] = jnp.broadcast_to(peak, top.shape)
    o_t[...] = jnp.zeros_like(o_t)

    def second_pass(k, masked):
        values_t = jnp.concatenate(
            [jnp.transpose(values[k]), jnp.ones((16, 512), BF)], axis=0
        )
        scores = dot(keys[k], q_t[...], NN) * SCALE - top[0:1, :]
        if masked:
            scores = jnp.where(hidden(k), FLOOR, scores)
        weights = jnp.exp2(scores).astype(BF)
        probs[k] = weights
        o_t[...] += dot(values_t, weights, NN)

    def second_step(d):
        kv_ahead(1, d + 1)

        @pl.when(d <= chip)
        def _():
            kv_arrived(1, d)
            second_pass(chip - d, False)

        @pl.when(d == 2)
        def _():
            arrive_all(near_arrivals(1))
            start_all(half_sends(1))
            arrive_all(x_arrivals(0))
            start_all(cross_sends(0))
            arrive_all(x_arrivals(1))
            start_all(cross_sends(1))

        @pl.when(d == 5)
        def _():
            arrive_all(half_arrivals(0))
            start_all(far_sends(0))

    kv_arrived(1, 0)
    second_pass(chip, True)
    loop_from(1, CHIPS, second_step)
    arrive_all(half_arrivals(1))
    start_all(far_sends(1))

    def project(slot, fresh=False):
        columns = pl.ds(pl.multiple_of(slot * WIDE, WIDE), WIDE)
        term = dot(w_ref[:, columns], picked[slot], NT)
        if fresh:
            g_t[...] = term
        else:
            g_t[...] += term

    w_copy.wait()
    project(t, True)
    project(z_down)
    project(z_up)
    project(x_far)
    project(z_far)
    arrive_all(cross_arrivals(0) + cross_arrivals(1))
    project(z_down + other)
    project(z_up + other)
    arrive_all(far_arrivals(0) + far_arrivals(1))
    project(z_far + other)

    router_row = router_ref[...]
    router_sum = jnp.zeros((1, ROWS), F32)
    for n in range(GROUP):
        lanes = slice(n * ROWS, (n + 1) * ROWS)
        g = g_t[n * HD : (n + 1) * HD, :]
        inverse = 1.0 / o_t[HD : HD + 1, lanes]
        share = jnp.sum(g * o_t[0:HD, lanes], axis=0, keepdims=True) * inverse
        router_sum += share
        level = router_row * inverse
        delta[0:1, lanes] = share * level
        scaled = g * level
        do_t[:, lanes] = scaled.astype(BF)
        do_s[lanes, :] = jnp.transpose(scaled).astype(BF)
    router_part[t] = jnp.broadcast_to(router_sum, (8, ROWS))

    def router_copy(step, slot):
        part = router_part.at[slot]
        return remote(
            part, part, router_send.at[step], router_recv.at[slot], (s, (t + step) % TP)
        )

    for step in range(1, TP):
        router_copy(step, t).start()

    def fold_copy(k):
        return remote(
            out_side.at[k], in_side.at[k], fold_send.at[k], fold_recv.at[k], (sibling, t)
        )

    def part_copy(k, source):
        return remote(
            out_part.at[k],
            in_part.at[source],
            part_send.at[k],
            part_recv.at[source],
            (k * 2 + core, t),
        )

    def backward_step(k):
        weights = probs[k]
        grad_probs = dot(values[k], do_t[...], NN) - delta[0:1, :]
        grad_scores = (weights.astype(F32) * grad_probs).astype(BF)
        acc[k, 1] = dot(weights, do_s[...], NN)
        acc[k, 0] = dot(grad_scores, q_s[...], NN)
        probs[k] = grad_scores
        for n in range(2):
            out_side[k, n] = acc[k, n, theirs, :].astype(BF)
        fold_copy(k).start()

    def fold(k):
        fold_copy(k).wait_recv()
        for n in range(2):
            acc[k, n, mine, :] += in_side[k, n].astype(F32)

    def pass_on(k):
        fold(k)
        for n in range(2):
            out_part[k, n] = acc[k, n, mine, :].astype(BF)
        part_copy(k, chip).start()

    def backward(k):
        backward_step(k)

        @pl.when(k > 1)
        def _():
            pass_on(k - 2)

    loop(chip + 1, backward)

    @pl.when(chip > 0)
    def _():
        pass_on(chip - 1)

    dq_t[...] = jnp.zeros_like(dq_t)

    def query_step(k):
        dq_t[...] += dot(keys[k], probs[k], TN)

    loop(chip + 1, query_step)
    for n in range(GROUP):
        block = jnp.transpose(dq_t[:, n * ROWS : (n + 1) * ROWS]) * FACTOR
        dq_ref[:, n * HD : (n + 1) * HD] = block.astype(BF)

    router_total = router_part[t]
    for step in range(1, TP):
        slot = (t + step) % TP
        router_copy(step, slot).wait_recv()
        router_total += router_part[slot]
    gr_ref[...] = router_total

    fold(chip)

    def collect(n):
        source = CHIPS - 1 - n

        @pl.when(source > chip)
        def _():
            part_copy(chip, source).wait_recv()
            for i in range(2):
                acc[chip, i, mine, :] += in_part[source, i].astype(F32)

    loop(CHIPS, collect)
    dk_ref[...] = (acc[chip, 0, mine, :] * FACTOR).astype(BF)
    dv_ref[...] = acc[chip, 1, mine, :].astype(BF)

    for i in range(2):
        later_chips(i, lambda copy: copy.wait_send())
    for c in range(2):
        for copy in own_sends(c) + half_sends(c) + cross_sends(c) + far_sends(c):
            copy.wait_send()
    for step in range(1, TP):
        router_copy(step, t).wait_send()

    def sent(k):
        @pl.when(k <= chip)
        def _():
            side_copy(0, k).wait_send()
            side_copy(1, k).wait_send()
            fold_copy(k).wait_send()

        @pl.when(k < chip)
        def _():
            part_copy(k, chip).wait_send()

    loop(CHIPS, sent)


def place(dq_in, dk_in, dv_in, gr_in, dq_ref, dk_ref, dv_ref, gr_ref, sem):
    copies = [
        pltpu.make_async_copy(dq_in, dq_ref, sem.at[0]),
        pltpu.make_async_copy(dk_in, dk_ref, sem.at[1]),
        pltpu.make_async_copy(dv_in, dv_ref, sem.at[2]),
    ]
    for copy in copies:
        copy.start()
    gr_ref[...] = gr_in[0:1, :]
    for copy in copies:
        copy.wait()


def body(grad_out, select, router, query, key_rows, value_rows, out_weight):
    vmem = pl.BlockSpec(memory_space=pltpu.VMEM)
    hbm = pl.BlockSpec(memory_space=pl.ANY)
    dma = pltpu.SemaphoreType.DMA
    shapes = (
        jax.ShapeDtypeStruct((ROWS, WIDE), BF),
        jax.ShapeDtypeStruct((ROWS, HD), BF),
        jax.ShapeDtypeStruct((ROWS, HD), BF),
    )
    parts = pl.pallas_call(
        kernel,
        out_shape=shapes + (jax.ShapeDtypeStruct((8, ROWS), F32),),
        in_specs=[hbm, hbm] + [vmem] * 5,
        out_specs=(vmem,) * 4,
        scratch_shapes=[
            pltpu.VMEM((CHIPS, 512, LANES), BF),
            pltpu.VMEM((WIDE, TP * WIDE), BF),
            pltpu.VMEM((TP, ROWS, WIDE), BF),
            pltpu.VMEM((CHIPS, 512, HD), BF),
            pltpu.VMEM((CHIPS, 512, HD), BF),
            pltpu.VMEM((CHIPS, 2, 512, HD), F32),
            pltpu.VMEM((CHIPS, 2, ROWS, HD), BF),
            pltpu.VMEM((CHIPS, 2, ROWS, HD), BF),
            pltpu.VMEM((CHIPS, 2, ROWS, HD), BF),
            pltpu.VMEM((CHIPS, 2, ROWS, HD), BF),
            pltpu.VMEM((HD, LANES), BF),
            pltpu.VMEM((LANES, HD), BF),
            pltpu.VMEM((8, LANES), F32),
            pltpu.VMEM((HD + 16, LANES), F32),
            pltpu.VMEM((WIDE, ROWS), F32),
            pltpu.VMEM((HD, LANES), BF),
            pltpu.VMEM((LANES, HD), BF),
            pltpu.VMEM((8, LANES), F32),
            pltpu.VMEM((HD, LANES), F32),
            pltpu.VMEM((TP, 8, ROWS), F32),
            dma((5,)),
            dma((2, CHIPS)),
            dma((2, SEQ)),
            dma((2, CHIPS)),
            dma((2, 8)),
            dma((2, 8)),
            dma((CHIPS,)),
            dma((CHIPS,)),
            dma((CHIPS,)),
            dma((CHIPS,)),
            dma((TP,)),
            dma((TP,)),
        ],
        compiler_params=pltpu.CompilerParams(
            collective_id=0, has_side_effects=True, vmem_limit_bytes=62 << 20
        ),
    )(
        grad_out,
        out_weight,
        select.reshape(1, ROWS),
        router.reshape(1, ROWS),
        query,
        key_rows,
        value_rows,
    )
    dq, dk, dv, gr = pl.pallas_call(
        place,
        out_shape=shapes + (jax.ShapeDtypeStruct((1, ROWS), F32),),
        in_specs=[vmem] * 4,
        out_specs=(hbm,) * 3 + (vmem,),
        scratch_shapes=[dma((3,))],
    )(*parts)
    return dq, dk, dv, gr.reshape(ROWS)


def solution(mesh):
    return jax.shard_map(
        body,
        mesh=mesh,
        in_specs=(
            P("seq", "tp"),
            P("seq"),
            P("seq"),
            P("seq", "tp"),
            P("seq", "tp"),
            P("seq", "tp"),
            P("tp", None),
        ),
        out_specs=(P("seq", "tp"), P("seq", "tp"), P("seq", "tp"), P("seq")),
        check_vma=False,
    )
```

time: 102 us -> 77.3 us (0.76)
  the two profiles are of different devices: /device:TPU:19 before, /device:TPU:15 now
where the time goes in v2:
time: 77.3 us; the launch traced here: 77.1 us
  Pallas kernels  76.5 us (99%)
    pallas_call x1, Pallas kernels, body(): pl.pallas_call(kernel, out_shape=shapes + (jax.ShapeDtypeStruct((8, ROWS)...  74 us
    pallas_call x1, Pallas kernels, body(): pl.pallas_call(place, out_shape=shapes + (jax.ShapeDtypeStruct((1, ROWS),...  2.5 us

profile of v2, /device:TPU:15, one launch (start us, length us, event | category | flops | bytes accessed | tf_op | source)
XLA Modules:
  0.0 77.1 jit_solution(15728289088385521456)
XLA Ops:
  0.6 74.0 %shard_map.102 = (bf16[256,1024]{1,0:T(8,128)(2,1)}, bf16[256,128]{1,0:T(8,128)(2,1)}, bf16[256,128]{1,0:T(8,128)(2,1)}, f32[8,256]{1,0:T(8,128)}) custom-call(bf16[2048,1024]{1,0:T(8,128)(2,1)} %go_hbm.1, bf16[1024,8192]{1,0:T(8,128)(2,1)} %w_hbm.1, s32[1,256]{1,0:T(1,128)} %bitcast.3, f32[1,256]{1,0:T(1,128)} %bitcast.4, bf16[256,1024]{1,0:T(8,128)(2,1)} %q_ref.1, ...), custom_call_target="tpu_custom_call" | custom-call | tf_op jit(solution)/shard_map/pallas_call | solution.py:513
  74.6 2.5 %shard_map.103 = (bf16[256,1024]{1,0:T(8,128)(2,1)}, bf16[256,128]{1,0:T(8,128)(2,1)}, bf16[256,128]{1,0:T(8,128)(2,1)}, f32[1,256]{1,0:T(1,128)}) custom-call(bf16[256,1024]{1,0:T(8,128)(2,1)} %get-tuple-element.12.dq_in, bf16[256,128]{1,0:T(8,128)(2,1)} %get-tuple-element.13.dk_in, bf16[256,128]{1,0:T(8,128)(2,1)} %get-tuple-element.14.dv_in, ...), custom_call_target="tpu_custom_call" | custom-call | tf_op jit(solution)/shard_map/pallas_call | solution.py:564

commit v3 on v2

--- a/solution.py
+++ b/solution.py
@@ -53,9 +53,9 @@
     w_hbm,
     sel_ref,
     router_ref,
-    q_ref,
-    k_ref,
-    v_ref,
+    q_hbm,
+    k_hbm,
+    v_hbm,
     dq_ref,
     dk_ref,
     dv_ref,
@@ -70,6 +70,7 @@
     in_side,
     out_part,
     in_part,
+    q_ref,
     q_t,
     q_s,
     top,
@@ -118,6 +119,14 @@
             device_id_type=MESH,
         )
 
+    mine = pl.ds(pl.multiple_of(core * ROWS, ROWS), ROWS)
+    theirs = pl.ds(pl.multiple_of((1 - core) * ROWS, ROWS), ROWS)
+    kv_inputs = [
+        pltpu.make_async_copy(k_hbm, keys.at[chip, mine, :], local_sem.at[5]),
+        pltpu.make_async_copy(v_hbm, values.at[chip, mine, :], local_sem.at[6]),
+    ]
+    for copy in kv_inputs:
+        copy.start()
     go_copies = []
     for p in range(4):
         go_copies.append(
@@ -130,7 +139,8 @@
     for copy in go_copies:
         copy.start()
     w_copy = pltpu.make_async_copy(w_hbm, w_ref, local_sem.at[4])
-    w_copy.start()
+    q_copy = pltpu.make_async_copy(q_hbm, q_ref, local_sem.at[7])
+    q_copy.start()
 
     barrier = pltpu.get_barrier_semaphore()
     pl.semaphore_signal(barrier, inc=1, device_id=(sibling, t), device_id_type=MESH)
@@ -145,10 +155,6 @@
         pl.semaphore_signal(
             barrier, inc=1, device_id=(s, (t + step) % TP), device_id_type=MESH
         )
-    mine = pl.ds(pl.multiple_of(core * ROWS, ROWS), ROWS)
-    theirs = pl.ds(pl.multiple_of((1 - core) * ROWS, ROWS), ROWS)
-    keys[chip, mine, :] = k_ref[...]
-    values[chip, mine, :] = v_ref[...]
 
     def choose(c):
         sel_half = jnp.transpose(
@@ -167,6 +173,8 @@
     for copy in go_copies:
         copy.wait()
     choose(0)
+    for copy in kv_inputs:
+        copy.wait()
     pl.semaphore_wait(barrier, CHIPS + TP - 1)
 
     def block_of(i, block):
@@ -258,9 +266,10 @@
 
     start_all(own_sends(0))
     choose(1)
-    start_all(own_sends(1))
+    w_copy.start()
     later_chips(1, lambda copy: copy.start())
 
+    q_copy.wait()
     for n in range(GROUP):
         block = q_ref[:, n * HD : (n + 1) * HD]
         q_s[n * ROWS : (n + 1) * ROWS, :] = block
@@ -287,14 +296,15 @@
             kv_arrived(0, d)
             first_pass(chip - d, False)
 
-        @pl.when(d == 5)
+        @pl.when(d == 2)
         def _():
             arrive_all(near_arrivals(0))
             start_all(half_sends(0))
 
+    start_all(own_sends(1))
     kv_arrived(0, 0)
+    first_pass(chip, True)
     kv_ahead(0, 1)
-    first_pass(chip, True)
     loop_from(1, CHIPS, first_step)
     kv_ahead(1, 1)
 
@@ -321,25 +331,24 @@
             kv_arrived(1, d)
             second_pass(chip - d, False)
 
-        @pl.when(d == 2)
-        def _():
-            arrive_all(near_arrivals(1))
-            start_all(half_sends(1))
-            arrive_all(x_arrivals(0))
-            start_all(cross_sends(0))
-            arrive_all(x_arrivals(1))
-            start_all(cross_sends(1))
-
-        @pl.when(d == 5)
+        @pl.when(d == 1)
         def _():
             arrive_all(half_arrivals(0))
             start_all(far_sends(0))
 
+        @pl.when(d == 2)
+        def _():
+            arrive_all(half_arrivals(1))
+            start_all(far_sends(1))
+
+    arrive_all(near_arrivals(1))
+    start_all(half_sends(1))
+    for c in range(2):
+        arrive_all(x_arrivals(c))
+        start_all(cross_sends(c))
     kv_arrived(1, 0)
     second_pass(chip, True)
     loop_from(1, CHIPS, second_step)
-    arrive_all(half_arrivals(1))
-    start_all(far_sends(1))
 
     def project(slot, fresh=False):
         columns = pl.ds(pl.multiple_of(slot * WIDE, WIDE), WIDE)
@@ -424,15 +433,11 @@
     def backward(k):
         backward_step(k)
 
-        @pl.when(k > 1)
-        def _():
-            pass_on(k - 2)
+        @pl.when(k > 0)
+        def _():
+            pass_on(k - 1)
 
     loop(chip + 1, backward)
-
-    @pl.when(chip > 0)
-    def _():
-        pass_on(chip - 1)
 
     dq_t[...] = jnp.zeros_like(dq_t)
 
@@ -513,7 +518,7 @@
     parts = pl.pallas_call(
         kernel,
         out_shape=shapes + (jax.ShapeDtypeStruct((8, ROWS), F32),),
-        in_specs=[hbm, hbm] + [vmem] * 5,
+        in_specs=[hbm, hbm, vmem, vmem, hbm, hbm, hbm],
         out_specs=(vmem,) * 4,
         scratch_shapes=[
             pltpu.VMEM((CHIPS, 512, LANES), BF),
@@ -526,6 +531,7 @@
             pltpu.VMEM((CHIPS, 2, ROWS, HD), BF),
             pltpu.VMEM((CHIPS, 2, ROWS, HD), BF),
             pltpu.VMEM((CHIPS, 2, ROWS, HD), BF),
+            pltpu.VMEM((ROWS, WIDE), BF),
             pltpu.VMEM((HD, LANES), BF),
             pltpu.VMEM((LANES, HD), BF),
             pltpu.VMEM((8, LANES), F32),
@@ -536,7 +542,7 @@
             pltpu.VMEM((8, LANES), F32),
             pltpu.VMEM((HD, LANES), F32),
             pltpu.VMEM((TP, 8, ROWS), F32),
-            dma((5,)),
+            dma((8,)),
             dma((2, CHIPS)),
             dma((2, SEQ)),
             dma((2, CHIPS)),

time: 77.3 us -> 70.6 us (0.913)
  the two profiles are of different devices: /device:TPU:15 before, /device:TPU:22 now
where the time goes in v3:
time: 70.6 us; the launch traced here: 70.5 us
  Pallas kernels  69.8 us (99%)
    pallas_call x1, Pallas kernels, body(): pl.pallas_call(kernel, out_shape=shapes + (jax.ShapeDtypeStruct((8, ROWS)...  67.3 us
    pallas_call x1, Pallas kernels, body(): pl.pallas_call(place, out_shape=shapes + (jax.ShapeDtypeStruct((1, ROWS),...  2.5 us

profile of v3, /device:TPU:22, one launch (start us, length us, event | category | flops | bytes accessed | tf_op | source)
XLA Modules:
  0.0 70.5 jit_solution(11887635475504586700)
XLA Ops:
  0.6 67.3 %shard_map.102 = (bf16[256,1024]{1,0:T(8,128)(2,1)}, bf16[256,128]{1,0:T(8,128)(2,1)}, bf16[256,128]{1,0:T(8,128)(2,1)}, f32[8,256]{1,0:T(8,128)}) custom-call(bf16[2048,1024]{1,0:T(8,128)(2,1)} %go_hbm.1, bf16[1024,8192]{1,0:T(8,128)(2,1)} %w_hbm.1, s32[1,256]{1,0:T(1,128)} %bitcast.3, f32[1,256]{1,0:T(1,128)} %bitcast.4, bf16[256,1024]{1,0:T(8,128)(2,1)} %q_hbm.1, ...), custom_call_target="tpu_custom_call" | custom-call | tf_op jit(solution)/shard_map/pallas_call | solution.py:518
  68.0 2.5 %shard_map.103 = (bf16[256,1024]{1,0:T(8,128)(2,1)}, bf16[256,128]{1,0:T(8,128)(2,1)}, bf16[256,128]{1,0:T(8,128)(2,1)}, f32[1,256]{1,0:T(1,128)}) custom-call(bf16[256,1024]{1,0:T(8,128)(2,1)} %get-tuple-element.12.dq_in, bf16[256,128]{1,0:T(8,128)(2,1)} %get-tuple-element.13.dk_in, bf16[256,128]{1,0:T(8,128)(2,1)} %get-tuple-element.14.dv_in, ...), custom_call_target="tpu_custom_call" | custom-call | tf_op jit(solution)/shard_map/pallas_call | solution.py:570

commit v4 on v3

--- a/solution.py
+++ b/solution.py
@@ -162,6 +162,8 @@
         )
         total = jnp.zeros((HALF, WIDE), F32)
         for p in range(4):
+            if c == 0:
+                go_copies[p].wait()
             pieces = []
             for b in range(4):
                 token = lax.broadcasted_iota(jnp.int32, (HALF, HALF), 1) + (p * 512 + b * 128)
@@ -170,8 +172,6 @@
             total += dot(chosen, probs[p // 2, :, (p % 2) * WIDE : (p % 2 + 1) * WIDE], NN)
         picked[t, c * HALF : (c + 1) * HALF, :] = total.astype(BF)
 
-    for copy in go_copies:
-        copy.wait()
     choose(0)
     for copy in kv_inputs:
         copy.wait()
@@ -430,12 +430,20 @@
             out_part[k, n] = acc[k, n, mine, :].astype(BF)
         part_copy(k, chip).start()
 
-    def backward(k):
-        backward_step(k)
-
-        @pl.when(k > 0)
-        def _():
-            pass_on(k - 1)
+    def turn(i):
+        after = (i + 4) // 6
+        to_y = (1 - after) + after * 2 * ((i + 1) % 2)
+        across = (1 - after) * (1 - i % 2) + after * (1 - i // 4)
+        ordered = to_y * 2 + (xl + across) % 2
+        last = i // 6
+        return (y // 3) * ((1 - last) * ordered + last * i) + (1 - y // 3) * i
+
+    def backward(i):
+        backward_step(turn(i))
+
+        @pl.when(i > 0)
+        def _():
+            pass_on(turn(i - 1))
 
     loop(chip + 1, backward)
 
@@ -458,9 +466,7 @@
 
     fold(chip)
 
-    def collect(n):
-        source = CHIPS - 1 - n
-
+    def collect(source):
         @pl.when(source > chip)
         def _():
             part_copy(chip, source).wait_recv()

time: 70.6 us -> 68.2 us (0.966)
  the two profiles are of different devices: /device:TPU:22 before, /device:TPU:1 now
where the time goes in v4:
time: 68.2 us; the launch traced here: 68 us
  Pallas kernels  67.4 us (99%)
    pallas_call x1, Pallas kernels, body(): pl.pallas_call(kernel, out_shape=shapes + (jax.ShapeDtypeStruct((8, ROWS)...  64.9 us
    pallas_call x1, Pallas kernels, body(): pl.pallas_call(place, out_shape=shapes + (jax.ShapeDtypeStruct((1, ROWS),...  2.5 us

profile of v4, /device:TPU:1, one launch (start us, length us, event | category | flops | bytes accessed | tf_op | source)
XLA Modules:
  0.0 68.0 jit_solution(4318098283584332431)
XLA Ops:
  0.6 64.9 %shard_map.102 = (bf16[256,1024]{1,0:T(8,128)(2,1)}, bf16[256,128]{1,0:T(8,128)(2,1)}, bf16[256,128]{1,0:T(8,128)(2,1)}, f32[8,256]{1,0:T(8,128)}) custom-call(bf16[2048,1024]{1,0:T(8,128)(2,1)} %go_hbm.1, bf16[1024,8192]{1,0:T(8,128)(2,1)} %w_hbm.1, s32[1,256]{1,0:T(1,128)} %bitcast.3, f32[1,256]{1,0:T(1,128)} %bitcast.4, bf16[256,1024]{1,0:T(8,128)(2,1)} %q_hbm.1, ...), custom_call_target="tpu_custom_call" | custom-call | tf_op jit(solution)/shard_map/pallas_call | solution.py:524
  65.5 2.5 %shard_map.103 = (bf16[256,1024]{1,0:T(8,128)(2,1)}, bf16[256,128]{1,0:T(8,128)(2,1)}, bf16[256,128]{1,0:T(8,128)(2,1)}, f32[1,256]{1,0:T(1,128)}) custom-call(bf16[256,1024]{1,0:T(8,128)(2,1)} %get-tuple-element.12.dq_in, bf16[256,128]{1,0:T(8,128)(2,1)} %get-tuple-element.13.dk_in, bf16[256,128]{1,0:T(8,128)(2,1)} %get-tuple-element.14.dv_in, ...), custom_call_target="tpu_custom_call" | custom-call | tf_op jit(solution)/shard_map/pallas_call | solution.py:576

commit v5 on v4

--- a/solution.py
+++ b/solution.py
@@ -380,9 +380,9 @@
         router_sum += share
         level = router_row * inverse
         delta[0:1, lanes] = share * level
-        scaled = g * level
-        do_t[:, lanes] = scaled.astype(BF)
-        do_s[lanes, :] = jnp.transpose(scaled).astype(BF)
+        scaled = (g * level).astype(BF)
+        do_t[:, lanes] = scaled
+        do_s[lanes, :] = jnp.transpose(scaled)
     router_part[t] = jnp.broadcast_to(router_sum, (8, ROWS))
 
     def router_copy(step, slot):
@@ -454,8 +454,8 @@
 
     loop(chip + 1, query_step)
     for n in range(GROUP):
-        block = jnp.transpose(dq_t[:, n * ROWS : (n + 1) * ROWS]) * FACTOR
-        dq_ref[:, n * HD : (n + 1) * HD] = block.astype(BF)
+        block = (dq_t[:, n * ROWS : (n + 1) * ROWS] * FACTOR).astype(BF)
+        dq_ref[:, n * HD : (n + 1) * HD] = jnp.transpose(block)
 
     router_total = router_part[t]
     for step in range(1, TP):

time: 68.2 us -> 68.2 us (level)
  no operation moved by 1% of the time
where the time goes in v5:
time: 68.2 us; the launch traced here: 68 us
  Pallas kernels  67.4 us (99%)
    pallas_call x1, Pallas kernels, body(): pl.pallas_call(kernel, out_shape=shapes + (jax.ShapeDtypeStruct((8, ROWS)...  64.9 us
    pallas_call x1, Pallas kernels, body(): pl.pallas_call(place, out_shape=shapes + (jax.ShapeDtypeStruct((1, ROWS),...  2.5 us

profile of v5, /device:TPU:1, one launch (start us, length us, event | category | flops | bytes accessed | tf_op | source)
XLA Modules:
  0.0 68.0 jit_solution(17778320200306665711)
XLA Ops:
  0.6 64.9 %shard_map.102 = (bf16[256,1024]{1,0:T(8,128)(2,1)}, bf16[256,128]{1,0:T(8,128)(2,1)}, bf16[256,128]{1,0:T(8,128)(2,1)}, f32[8,256]{1,0:T(8,128)}) custom-call(bf16[2048,1024]{1,0:T(8,128)(2,1)} %go_hbm.1, bf16[1024,8192]{1,0:T(8,128)(2,1)} %w_hbm.1, s32[1,256]{1,0:T(1,128)} %bitcast.3, f32[1,256]{1,0:T(1,128)} %bitcast.4, bf16[256,1024]{1,0:T(8,128)(2,1)} %q_hbm.1, ...), custom_call_target="tpu_custom_call" | custom-call | tf_op jit(solution)/shard_map/pallas_call | solution.py:524
  65.5 2.5 %shard_map.103 = (bf16[256,1024]{1,0:T(8,128)(2,1)}, bf16[256,128]{1,0:T(8,128)(2,1)}, bf16[256,128]{1,0:T(8,128)(2,1)}, f32[1,256]{1,0:T(1,128)}) custom-call(bf16[256,1024]{1,0:T(8,128)(2,1)} %get-tuple-element.12.dq_in, bf16[256,128]{1,0:T(8,128)(2,1)} %get-tuple-element.13.dk_in, bf16[256,128]{1,0:T(8,128)(2,1)} %get-tuple-element.14.dv_in, ...), custom_call_target="tpu_custom_call" | custom-call | tf_op jit(solution)/shard_map/pallas_call | solution.py:576
